TPU v7x, 512 devices: a whole 4x4x16 slice. The times are simulated.
512 devices in a mesh: dp: 64 (over z, y), section: 8 (over x, core).
Axes of the slice: x: 4, y: 4, z: 16, core: 2. Of those that a mesh axis runs over, the one named last changes fastest.
Arguments:
- section_rows: bfloat16 [8, 8192, 2048], P('section', 'dp'), may hold values from -16 to 16
- embedded: bfloat16 [8192, 2048], P('dp'), may hold values from -16 to 16
- norm_gain: float32 [8, 1024], P('section'), may hold values from 0.1 to 1.9
- routes: int32 [8, 8192, 6], P('section', 'dp'), may hold values from 0 to 63, all different within a row; in each aligned block of 128 rows (0 to 127, 128 to 255, ..., all dimensions but the last counted through in order) at most 16 rows name the same one
- out_grad: bfloat16 [8, 8192, 6, 704], P('section', 'dp'), may hold values from -6 to 6
- momentum: bfloat16 [8, 64, 1024, 704], P('section', None, 'dp'), may hold values from -120 to 120
Outputs:
- update: bfloat16 [8, 64, 1024, 704], P('section', None, 'dp')
Inputs may be any that keep to these rules, and one draw needn't show every extreme that they name: `routes`: among the rows of one device no expert is named by more than 16 of its slots; some expert is named by exactly 16 in some of them.
All inputs are finite; a program needn't handle non-finite values.
Results may differ from a plain program's by a relative error of at most 0.018.
Values may be sent and summed in bfloat16 or wider, within the bound.
A program may use at most 64 MiB of HBM per device.

v0:
```python
import math

import jax
import jax.numpy as jnp
from jax import lax
from jax.sharding import PartitionSpec as P

NS_ITERS = 2


COEF_A = 3.4445
COEF_B = -4.775
COEF_C = 2.0315
MOMENTUM_RATE = 0.95
NORM_EPS = 1e-06


def from_behind(block, axis, distance):
    devices = range(lax.axis_size(axis))
    route = [(i - distance, i) for i in devices if i - distance in devices]
    return lax.ppermute(block, axis, route)


def window_features(rows, gain_row):
    values = rows.astype(jnp.float32)
    inverse = lax.rsqrt(jnp.mean(values * values, axis=-1, keepdims=True) + NORM_EPS)
    width = gain_row.shape[-1]
    return (values[:, :width] * inverse * gain_row).astype(jnp.bfloat16)


def newton_schulz(gradient, momentum_rows):
    blended = gradient + MOMENTUM_RATE * (
        MOMENTUM_RATE * momentum_rows.astype(jnp.float32) + gradient
    )
    frobenius = jnp.sqrt(jnp.sum(blended * blended))
    iterate = (blended / (frobenius + 1e-07)).astype(jnp.bfloat16)
    for repeat in range(NS_ITERS):
        gram = lax.dot_general(
            iterate, iterate, (((0,), (0,)), ((), ())), preferred_element_type=jnp.float32
        ).astype(jnp.bfloat16)
        squared = jnp.dot(gram, gram, preferred_element_type=jnp.float32)
        polynomial = (COEF_B * gram.astype(jnp.float32) + COEF_C * squared).astype(jnp.bfloat16)
        iterate = (
            COEF_A * iterate.astype(jnp.float32)
            + jnp.dot(iterate, polynomial, preferred_element_type=jnp.float32)
        ).astype(jnp.bfloat16)
    factor = 0.2 * math.sqrt(iterate.shape[0])
    return (factor * iterate.astype(jnp.float32)).astype(jnp.bfloat16)


def on_device(section_rows, embedded, norm_gain, routes, out_grad, momentum):
    peers = lax.axis_size("dp")
    section_index = lax.axis_index("section")
    received = from_behind(section_rows[0], "section", 1)
    layer_input = jnp.where(section_index == 0, embedded, received)
    features = window_features(layer_input, norm_gain[0])
    tokens_here = routes.shape[1]
    top_count = routes.shape[2]
    width_rows = features.shape[1]
    width_hidden = out_grad.shape[3]
    capacity = max(2, 4 * tokens_here * top_count // (3 * peers))
    owner = routes[0].reshape(-1)
    onehot = (owner[:, None] == jnp.arange(peers, dtype=jnp.int32)[None, :]).astype(jnp.int32)
    position = jnp.sum(onehot * (jnp.cumsum(onehot, axis=0) - 1), axis=1)
    target = owner * capacity + position
    token_of = jnp.arange(owner.shape[0], dtype=jnp.int32) // top_count
    send_rows = (
        jnp.zeros((peers * capacity, width_rows), jnp.bfloat16).at[target].set(features[token_of])
    )
    send_grads = (
        jnp.zeros((peers * capacity, width_hidden), jnp.bfloat16)
        .at[target]
        .set(out_grad[0].reshape(-1, width_hidden))
    )
    send_rows = send_rows.reshape(peers, capacity, width_rows)
    send_grads = send_grads.reshape(peers, capacity, width_hidden)
    got_rows, got_grads = (
        lax.all_to_all(send_rows, "dp", split_axis=0, concat_axis=0, tiled=True),
        lax.all_to_all(send_grads, "dp", split_axis=0, concat_axis=0, tiled=True),
    )
    owned = lax.all_to_all(momentum[0], "dp", split_axis=0, concat_axis=1, tiled=True)[0]
    gradient = lax.dot_general(
        got_rows, got_grads, (((0, 1), (0, 1)), ((), ())), preferred_element_type=jnp.float32
    )
    orthogonal = newton_schulz(gradient, owned)
    pieces = lax.all_to_all(orthogonal[None], "dp", split_axis=1, concat_axis=0, tiled=True)
    return pieces[None]


def solution(mesh):
    in_specs = (
        P("section", "dp", None),
        P("dp", None),
        P("section", None),
        P("section", "dp", None),
        P("section", "dp", None, None),
        P("section", None, "dp", None),
    )
    out_specs = P("section", None, "dp", None)
    return jax.shard_map(
        on_device, mesh=mesh, in_specs=in_specs, out_specs=out_specs, check_vma=False
    )
```

profile of v0, /device:TPU:2, one launch (start us, length us, event | category | flops | bytes accessed | tf_op | source)
XLA Modules:
  0.0 422.1 jit_solution(16001509724849907395)
XLA Ops:
  0.0 18.9 %all-to-all-start.2 = ((bf16[64,16,704]{2,1,0:T(8,128)(2,1)}), bf16[64,16,704]{2,1,0:T(8,128)(2,1)S(1)}, u32[]{:S(2)}, u32[]{:S(2)}) async-start(bf16[64,16,704]{2,1,0:T(8,128)(2,1)} %bitcast.46), calls=%async_computation.2 | async-start | bytes 3145728 | tf_op jit(solution)/shard_map/all_to_all | solution.py:81
  19.6 1.8 reduce-window.6
  21.7 2.1 copy.22
  25.5 7.5 %scatter_custom_fusion.1 = bf16[1024,704]{1,0:T(8,128)(2,1)} fusion(s32[768]{0:T(1024)S(1)} %fusion.12, bf16[768,704]{1,0:T(8,128)(2,1)} %reshape.137, bf16[]{:T(256)} %constant.18.clone.1), kind=kCustom, calls=%fused_computation.21 | custom fusion | bytes 1442304 | tf_op jit(solution)/shard_map/scatter | solution.py:73
  33.0 63.6 %all-to-all-done.2 = bf16[64,16,704]{2,1,0:T(8,128)(2,1)S(1)} async-done(((bf16[64,16,704]{2,1,0:T(8,128)(2,1)}), bf16[64,16,704]{2,1,0:T(8,128)(2,1)S(1)}, u32[]{:S(2)}, u32[]{:S(2)}) %all-to-all-start.2) | async-done | bytes 1441824 | tf_op jit(solution)/shard_map/all_to_all | solution.py:81
  97.8 5.8 %all-to-all-start.1 = ((bf16[64,16,704]{2,1,0:T(8,128)(2,1)}), bf16[64,16,704]{2,1,0:T(8,128)(2,1)S(1)}, u32[]{:S(2)}, u32[]{:S(2)}) async-start(bf16[64,16,704]{2,1,0:T(8,128)(2,1)} %bitcast.4), calls=%async_computation.1 | async-start | bytes 3145728 | tf_op jit(solution)/shard_map/all_to_all | solution.py:79
  103.6 2.1 collective-permute-start
  105.8 8.6 %collective-permute-done = bf16[128,2048]{1,0:T(8,128)(2,1)S(1)} collective-permute-done((bf16[128,2048]{1,0:T(8,128)(2,1)}, bf16[128,2048]{1,0:T(8,128)(2,1)S(1)}, u32[]{:S(2)}, u32[]{:S(2)}) %collective-permute-start) | collective-permute-done | bytes 524320 | tf_op jit(solution)/shard_map/ppermute | solution.py:21
  114.7 14.9 %scatter_custom_fusion = bf16[1024,1024]{1,0:T(8,128)(2,1)} fusion(s32[768]{0:T(1024)S(1)} %fusion.12, bf16[128,1024]{1,0:T(8,128)(2,1)S(1)} %fusion.8, s32[1024]{0:T(1024)S(1)} %pad_clamp_fusion, bf16[]{:T(256)} %constant.18.clone.1), kind=kCustom, calls=%fused_computation.14 | custom fusion | bytes 2097154 | tf_op jit(solution)/shard_map/scatter | solution.py:68
  129.7 51.2 %all-to-all-done.1 = bf16[64,16,704]{2,1,0:T(8,128)(2,1)S(1)} async-done(((bf16[64,16,704]{2,1,0:T(8,128)(2,1)}), bf16[64,16,704]{2,1,0:T(8,128)(2,1)S(1)}, u32[]{:S(2)}, u32[]{:S(2)}) %all-to-all-start.1) | async-done | bytes 1441824 | tf_op jit(solution)/shard_map/all_to_all | solution.py:79
  182.0 6.3 %all-to-all-start = ((bf16[64,16,1024]{2,1,0:T(8,128)(2,1)}), bf16[64,16,1024]{2,1,0:T(8,128)(2,1)}, u32[]{:S(2)}, u32[]{:S(2)}) async-start(bf16[64,16,1024]{2,1,0:T(8,128)(2,1)} %bitcast.3), calls=%async_computation | async-start | bytes 4194304 | tf_op jit(solution)/shard_map/all_to_all | solution.py:78
  188.3 1.8 convert_multiply_fusion
  190.2 2.3 copy.25
  192.5 95.1 %all-to-all-done = bf16[64,16,1024]{2,1,0:T(8,128)(2,1)} async-done(((bf16[64,16,1024]{2,1,0:T(8,128)(2,1)}), bf16[64,16,1024]{2,1,0:T(8,128)(2,1)}, u32[]{:S(2)}, u32[]{:S(2)}) %all-to-all-start) | async-done | bytes 2097184 | tf_op jit(solution)/shard_map/all_to_all | solution.py:78
  287.6 5.7 %multiply_reduce_fusion = (f32[]{:T(128)}, f32[1024,704]{0,1:T(8,128)S(1)}) fusion(f32[1024,704]{0,1:T(8,128)} %copy.25, bf16[64,16,1024]{2,1,0:T(8,128)(2,1)} %all-to-all-done, bf16[64,16,704]{2,1,0:T(8,128)(2,1)} %copy-done.1), kind=kOutput, calls=%fused_computation.11 | convolution fusion | flops 1479999488 | bytes 9306116 | tf_op jit(solution)/shard_map/dot_general | solution.py:82
  294.0 2.3 convolution_convert_fusion.1
  296.3 6.3 %add_convert_fusion.1 = bf16[1024,704]{0,1:T(8,128)(2,1)} fusion(bf16[704,704]{1,0:T(8,128)(2,1)} %convolution_convert_fusion.1, f32[1024,704]{0,1:T(8,128)S(1)} %get-tuple-element.8, f32[]{:T(128)S(6)} %add.85), kind=kOutput, calls=%fused_computation.9 | convolution fusion | flops 1721094144 | bytes 5316612 | tf_op jit(solution)/shard_map/dot_general | solution.py:45
  302.6 3.3 convolution_convert_fusion
  305.9 4.3 %fusion.3 = bf16[1,1024,704]{1,2,0:T(8,128)(2,1)} fusion(bf16[1024,704]{0,1:T(8,128)(2,1)S(1)} %copy-done.4, bf16[704,704]{1,0:T(8,128)(2,1)S(1)} %convolution_convert_fusion), kind=kOutput, calls=%fused_computation.18 | convolution fusion | flops 1720373248 | bytes 3874816 | tf_op jit(solution)/shard_map/dot_general | solution.py:45
  310.2 7.4 %copy.26 = bf16[1,1024,704]{2,0,1:T(2,128)(2,1)S(1)} copy(bf16[1,1024,704]{1,2,0:T(8,128)(2,1)} %fusion.3) | data formatting | bytes 2883584 | tf_op jit(solution)/shard_map/broadcast_in_dim | solution.py:86
  318.2 11.9 %reduce.6 = bf16[1024,704]{1,0:T(8,128)(2,1)} reduce(bf16[1024,1,704]{2,1,0:T(2,128)(2,1)S(1)} %bitcast.43, bf16[]{:T(256)} %broadcast.172), dimensions={1}, to_apply=%bitcast.30.reduce_sub_computation | reduce | bytes 2883586
  330.1 4.1 reshape.153
  334.2 76.5 %all_to_all.31 = bf16[64,2,5632]{2,1,0:T(2,128)(2,1)} all-to-all(bf16[64,2,5632]{2,1,0:T(2,128)(2,1)S(1)} %reshape.153), channel_id=1, replica_groups=mesh['dp'=64,'section'=8] {'dp'}, dimensions={0} | all-to-all | bytes 2883584 | tf_op jit(solution)/shard_map/all_to_all | solution.py:86
  410.7 9.6 %reshape.154 = bf16[1024,1,704]{2,1,0:T(2,128)(2,1)S(1)} reshape(bf16[64,2,5632]{2,1,0:T(2,128)(2,1)} %all_to_all.31) | data formatting | bytes 2883584
  (29 shorter events, 7.4 us)
Async XLA Ops:
  0.0 18.9 %copy-start.2 = (s32[1,128,6]{1,0,2:T(1,128)S(1)}, s32[1,128,6]{1,0,2:T(1,128)}, u32[]{:S(2)}) copy-start(s32[1,128,6]{1,0,2:T(1,128)} %param.9) | copy-start | bytes 9220
  0.0 96.6 %all-to-all-start.2 = ((bf16[64,16,704]{2,1,0:T(8,128)(2,1)}), bf16[64,16,704]{2,1,0:T(8,128)(2,1)S(1)}, u32[]{:S(2)}, u32[]{:S(2)}) async-start(bf16[64,16,704]{2,1,0:T(8,128)(2,1)} %bitcast.46), calls=%async_computation.2 | async-start | bytes 3145728 | tf_op jit(solution)/shard_map/all_to_all | solution.py:81
  96.6 1.1 copy-start
  97.8 83.1 %all-to-all-start.1 = ((bf16[64,16,704]{2,1,0:T(8,128)(2,1)}), bf16[64,16,704]{2,1,0:T(8,128)(2,1)S(1)}, u32[]{:S(2)}, u32[]{:S(2)}) async-start(bf16[64,16,704]{2,1,0:T(8,128)(2,1)} %bitcast.4), calls=%async_computation.1 | async-start | bytes 3145728 | tf_op jit(solution)/shard_map/all_to_all | solution.py:79
  103.6 11.0 %copy-start.3 = (f32[1,1024]{1,0:T(1,128)S(1)}, f32[1,1024]{1,0:T(1,128)}, u32[]{:S(2)}) copy-start(f32[1,1024]{1,0:T(1,128)} %param.8) | copy-start | bytes 12292
  103.6 10.7 %collective-permute-start = (bf16[128,2048]{1,0:T(8,128)(2,1)}, bf16[128,2048]{1,0:T(8,128)(2,1)S(1)}, u32[]{:S(2)}, u32[]{:S(2)}) collective-permute-start(bf16[128,2048]{1,0:T(8,128)(2,1)} %bitcast.49), channel_id=1, source_target_pairs={{0,1},{1,2},{2,3},{3,4},{4,5},{5,6},{6,7},{8,9},{9,10},{10,11},{11... | collective-permute-start | bytes 1572872 | tf_op jit(solution)/shard_map/ppermute | solution.py:21
  180.8 1.2 copy-start.1
  182.0 105.5 %all-to-all-start = ((bf16[64,16,1024]{2,1,0:T(8,128)(2,1)}), bf16[64,16,1024]{2,1,0:T(8,128)(2,1)}, u32[]{:S(2)}, u32[]{:S(2)}) async-start(bf16[64,16,1024]{2,1,0:T(8,128)(2,1)} %bitcast.3), calls=%async_computation | async-start | bytes 4194304 | tf_op jit(solution)/shard_map/all_to_all | solution.py:78
  302.6 3.3 copy-start.4
where the time goes:
time: 428 us; the launch traced here: 422 us
  waiting for transfers between devices  218 us (51%)
  blocking collectives  76.5 us (18%)
  local copies, waits for them, and re-layouts  54.7 us (13%)
  starting transfers between devices  33.1 us (8%)
  matrix products  21.9 us (5%)
  other arithmetic  16.2 us (4%)
    all_to_all x1, waiting for transfers between devices, on_device(): lax.all_to_all(send_rows, 'dp', split_axis=0, concat_axis=0, tiled=True)  95.1 us
    all_to_all x1, blocking collectives, on_device(): lax.all_to_all(orthogonal[None], 'dp', split_axis=1, concat_axis=0, tiled...  76.5 us
    all_to_all x1, waiting for transfers between devices, on_device(): lax.all_to_all(momentum[0], 'dp', split_axis=0, concat_axis=1, tiled=True)  63.6 us
    all_to_all x1, waiting for transfers between devices, on_device(): lax.all_to_all(send_grads, 'dp', split_axis=0, concat_axis=0, tiled=True)  51.2 us
    unnamed x16, local copies, waits for them, and re-layouts  20.2 us
    all_to_all x1, starting transfers between devices, on_device(): lax.all_to_all(momentum[0], 'dp', split_axis=0, concat_axis=1, tiled=True)  18.9 us
    scatter x1, local copies, waits for them, and re-layouts, on_device(): jnp.zeros((peers * capacity, width_rows), jnp.bfloat16).at[target]  14.9 us
    unnamed x1, other arithmetic  11.9 us
  transfers between devices with their start and end apart: 4, of which 4 were waited for; matrix products, arithmetic and copies ran while one was open for 8% of the time, Pallas kernels for 0%

commit v1 on v0

v1 whole, which is shorter than its diff:
```python
import functools
import math

import jax
import jax.numpy as jnp
from jax import lax
from jax.experimental import pallas as pl
from jax.experimental.pallas import tpu as pltpu
from jax.sharding import PartitionSpec as P

MESH = pl.DeviceIdType.MESH
F32 = jnp.float32
BF16 = jnp.bfloat16

NS_ITERS = 2
COEF_A = 3.4445
COEF_B = -4.775
COEF_C = 2.0315
MOMENTUM_RATE = 0.95
NORM_EPS = 1e-06

NY = 4
CAP = 16
PAD = 8
LANES = 128


def iota(shape, dim):
    return lax.broadcasted_iota(jnp.int32, shape, dim)


def kernel(
    n_dp,
    n_sec,
    rows_ref,
    emb_ref,
    gain_ref,
    routes_ref,
    gt_ref,
    mom_ref,
    out_ref,
    rrecv,
    fall,
    wk,
    pmsend,
    pmrecv,
    gsc,
    gsend,
    mrecv,
    grecv,
    ysend,
    frecv,
    bl,
    xs,
    gram,
    poly,
    upd,
    x_sem,
    m_sem,
    g_sem,
    p_sem,
    y_sem,
    u_sem,
    ring_send,
    ring_recv,
):
    nz = n_dp // NY
    half = nz // 2
    top, hidden, tokens = gt_ref.shape
    width = gain_ref.shape[1]
    block = mom_ref.shape[1]
    main = mrecv.shape[1]
    padded = grecv.shape[1]
    tail = hidden - main
    group = NY * CAP

    me = lax.axis_index("dp")
    sec = lax.axis_index("section")
    z = me // NY
    y = me % NY

    def wrap(index):
        return lax.rem(index + nz, nz)

    def remote(src, dst, sems, to_z, to_y):
        return pltpu.make_async_remote_copy(
            src_ref=src,
            dst_ref=dst,
            send_sem=sems.at[0],
            recv_sem=sems.at[1],
            device_id=(to_z * NY + to_y, sec),
            device_id_type=MESH,
        )

    def take(ref, sem):
        pltpu.make_async_copy(ref, ref, sem).wait()

    def rows_at(ref, start, size):
        return ref.at[pl.ds(pl.multiple_of(start, size), size)]

    barrier = pltpu.get_barrier_semaphore()
    after = lax.rem(sec + 1, n_sec)
    before = lax.rem(sec + n_sec - 1, n_sec)

    def greet(k, carry):
        pl.semaphore_signal(
            barrier, inc=1, device_id=(lax.rem(me + k, n_dp), sec), device_id_type=MESH
        )
        return carry

    lax.fori_loop(1, n_dp, greet, 0)
    for other in (after, before):
        pl.semaphore_signal(barrier, inc=1, device_id=(me, other), device_id_type=MESH)
    pl.semaphore_wait(barrier, n_dp + 1)

    section_copy = pltpu.make_async_remote_copy(
        src_ref=rows_ref,
        dst_ref=rrecv,
        send_sem=x_sem.at[0],
        recv_sem=x_sem.at[1],
        device_id=(me, after),
        device_id_type=MESH,
    )
    section_copy.start()

    same_parity = lax.rem(z, 2)

    def offset(phase, jz):
        near = half - 2 * ((jz + 1) // 2)
        near = jnp.where(jz % 2 == 1, near, -near)
        odd = half - 1 - 2 * (jz // 2)
        odd = jnp.where(jz % 2 == 0, odd, -odd)
        return jnp.where(same_parity == phase, near, odd)

    def send_to(src, dst, sems, to_z, to_y):
        target = to_z * NY + to_y

        @pl.when(target != me)
        def _():
            remote(src, dst, sems, to_z, to_y).start()

        @pl.when(target == me)
        def _():
            pltpu.make_async_copy(src, dst, sems.at[1]).start()

    def send_momentum(phase, lo, hi):
        def one(j, carry):
            to_z = wrap(z + offset(phase, j // NY))
            to_y = lax.rem(y + j % NY, NY)
            send_to(
                mom_ref.at[to_z * NY + to_y, :, pl.ds(0, main)],
                rows_at(mrecv, block * me, block),
                m_sem,
                to_z,
                to_y,
            )
            return carry

        lax.fori_loop(lo, hi, one, 0)

    send_momentum(0, 0, half * NY)

    table = nz * PAD
    expert = iota((table, tokens), 0)
    expert = jnp.where(expert % PAD < NY, (expert // PAD) * NY + expert % PAD, -1)
    named = jnp.zeros((table, tokens), F32)
    for k in range(top):
        named += jnp.where(routes_ref[k : k + 1, :] == expert, 1.0, 0.0)
    earlier = jnp.where(iota((tokens, tokens), 0) < iota((tokens, tokens), 1), 1.0, 0.0)
    place = jnp.dot(named.astype(BF16), earlier.astype(BF16), preferred_element_type=F32)
    for k in range(top):
        wk[k] = jnp.where(routes_ref[k : k + 1, :] == expert, place, -1.0).astype(BF16)
    pmsend[...] = jnp.where(named > 0.0, place, -1.0)

    def send_places(dz, carry):
        to_z = wrap(z + dz)
        send_to(rows_at(pmsend, PAD * to_z, PAD), rows_at(pmrecv, PAD * z, PAD), p_sem, to_z, y)
        return carry

    lax.fori_loop(0, nz, send_places, 0)

    for k in range(top):
        widened = jnp.concatenate(
            [gt_ref[k], jnp.zeros((padded - hidden, tokens), BF16)], axis=0
        )
        gsc[k * tokens : (k + 1) * tokens, :] = widened.T

    section_copy.wait_recv()
    values = jnp.where(sec == 0, emb_ref[...], rrecv[...]).astype(F32)
    inverse = lax.rsqrt(jnp.mean(values * values, axis=-1, keepdims=True) + NORM_EPS)
    fall[pl.ds(pl.multiple_of(z * tokens, tokens), tokens), :] = (
        values[:, :width] * inverse * gain_ref[...]
    ).astype(BF16)

    directions = ((0, 1, half), (1, -1, half - 1))

    def ring_copy(di, d, step):
        part = rows_at(fall, wrap(z - d * step) * tokens, tokens)
        return pltpu.make_async_remote_copy(
            src_ref=part,
            dst_ref=part,
            send_sem=ring_send.at[di, step],
            recv_sem=ring_recv.at[di, step],
            device_id=(wrap(z + d) * NY + y, sec),
            device_id_type=MESH,
        )

    def ring_step(step):
        for di, d, count in directions:
            if 1 <= step <= count:
                ring_copy(di, d, step - 1).wait_recv()
            if step < count:
                ring_copy(di, d, step).start()

    slots = 4 * group
    shift = jnp.where(
        iota((tail, LANES), 1) == iota((tail, LANES), 0) + (LANES - tail), 1.0, 0.0
    ).astype(BF16)
    chunks = half // 4

    def pack(phase, q):
        base = (phase * chunks + q) * slots
        to = [wrap(z + offset(phase, 4 * q + i)) for i in range(4)]
        which = iota((slots, table), 0)
        row = jnp.zeros((slots, table), jnp.int32)
        for i in range(4):
            row = jnp.where(which // group == i, to[i] * PAD, row)
        row = row + (which // CAP) % NY
        spread = jnp.where(iota((slots, table), 1) == row, 1.0, 0.0).astype(BF16)
        spot = (iota((slots, tokens), 0) % CAP).astype(F32)
        picks = []
        for k in range(top):
            at = jnp.dot(spread, wk[k], preferred_element_type=F32)
            picks.append(jnp.where(at == spot, 1.0, 0.0).astype(BF16))
        chosen = jnp.dot(jnp.concatenate(picks, axis=1), gsc[...], preferred_element_type=F32)
        gsend[base : base + slots, :main] = chosen[:, :main].astype(BF16)
        tails = jnp.concatenate(
            [
                mom_ref[pl.ds(to[i] * NY, NY), :, main:hidden].reshape(NY * block, tail)
                for i in range(4)
            ],
            axis=0,
        )
        gsend[base : base + slots, main:] = (
            chosen[:, main:] + jnp.dot(tails, shift, preferred_element_type=F32)
        ).astype(BF16)

        def one(j, carry):
            to_z = wrap(z + offset(phase, 4 * q + j // NY))
            to_y = j % NY
            send_to(
                rows_at(gsend, base + j * CAP, CAP),
                rows_at(grecv, CAP * me, CAP),
                g_sem,
                to_z,
                to_y,
            )
            return carry

        lax.fori_loop(0, 4 * NY, one, 0)

    def pick(source):
        places = pmrecv[pl.ds(pl.multiple_of(source * PAD, PAD), PAD), :]
        at = jnp.concatenate(
            [jnp.broadcast_to(places[i : i + 1, :], (CAP, tokens)) for i in range(NY)], axis=0
        )
        spot = (iota((group, tokens), 0) % CAP).astype(F32)
        chosen = jnp.dot(
            jnp.where(at == spot, 1.0, 0.0).astype(BF16),
            fall[pl.ds(pl.multiple_of(source * tokens, tokens), tokens), :],
            preferred_element_type=F32,
        )
        ysend[pl.ds(pl.multiple_of(source * group, group), group), :] = chosen.astype(BF16)
        for dy in range(NY):
            to_y = lax.rem(y + dy, NY)
            src = rows_at(ysend, source * group + to_y * CAP, CAP)
            dst = rows_at(frecv, (source * NY + y) * CAP, CAP)
            if dy == 0:
                pltpu.make_async_copy(src, dst, y_sem.at[1]).start()
            else:
                remote(src, dst, y_sem, z, to_y).start()

    def pick_step(step):
        pick(wrap(z + step))
        if 0 < step < half:
            pick(wrap(z - step))

    fillers = [functools.partial(pack, 0, q) for q in range(chunks)]
    fillers.append(functools.partial(send_momentum, 1, 0, half * NY))
    fillers += [functools.partial(pack, 1, q) for q in range(chunks)]
    slots_for = {1: 0, 3: 1, 5: 2, 6: 3, 7: 4}
    for step in range(half + 1):
        ring_step(step)
        if step == 0:
            take(pmrecv, p_sem.at[1])
        pick_step(step)
        for at_step, index in slots_for.items():
            if min(at_step, half) == step and index < len(fillers):
                fillers[index]()

    take(frecv, y_sem.at[1])
    take(grecv, g_sem.at[1])
    take(mrecv, m_sem.at[1])
    tile = 256
    tiles = width // tile

    def blend(t, total):
        rows = pl.ds(pl.multiple_of(t * tile, tile), tile)
        cols = pl.ds(pl.multiple_of(t * tile, tile), tile)
        gradient = lax.dot_general(
            frecv[:, cols], grecv[...], (((0,), (0,)), ((), ())), preferred_element_type=F32
        )

        def mixed(grad, mom):
            return grad + MOMENTUM_RATE * (MOMENTUM_RATE * mom + grad)

        first = mixed(gradient[:, :main], mrecv[rows, :].astype(F32))
        rest = pltpu.roll(grecv[rows, main:].astype(F32), tail, 1)
        last = mixed(gradient[:, main:], rest)
        last = jnp.where(iota(last.shape, 1) < tail, last, 0.0)
        bl[rows, :main] = first
        bl[rows, main:] = last
        return total + jnp.sum(first * first) + jnp.sum(last * last)

    total = lax.fori_loop(0, tiles, blend, jnp.zeros((), F32))
    scale = 1.0 / (jnp.sqrt(jnp.full((1, 1), total, F32)) + 1e-07)

    def normalize(t, carry):
        rows = pl.ds(pl.multiple_of(t * tile, tile), tile)
        xs[rows, :] = (bl[rows, :] * scale).astype(BF16)
        return carry

    lax.fori_loop(0, tiles, normalize, 0)

    factor = 0.2 * math.sqrt(width)
    for repeat in range(NS_ITERS):
        last_one = repeat == NS_ITERS - 1

        def make_gram(t, carry):
            cols = pl.ds(pl.multiple_of(t * tile, tile), tile)
            gram[cols, :] = lax.dot_general(
                xs[:, cols], xs[...], (((0,), (0,)), ((), ())), preferred_element_type=F32
            ).astype(BF16)
            return carry

        def make_poly(t, carry):
            rows = pl.ds(pl.multiple_of(t * tile, tile), tile)
            here = gram[rows, :]
            squared = jnp.dot(here, gram[...], preferred_element_type=F32)
            poly[rows, :] = (COEF_B * here.astype(F32) + COEF_C * squared).astype(BF16)
            return carry

        def make_iterate(k, carry):
            t = lax.rem(z // (tile // (NY * block)) + k, tiles)
            rows = pl.ds(pl.multiple_of(t * tile, tile), tile)
            here = xs[rows, :]
            fresh = (
                COEF_A * here.astype(F32) + jnp.dot(here, poly[...], preferred_element_type=F32)
            ).astype(BF16)
            if not last_one:
                xs[rows, :] = fresh
                return carry
            upd[rows, :] = (factor * fresh.astype(F32)).astype(BF16)[:, :hidden]

            def one(j, inner):
                target = t * (tile // block) + j
                send_to(
                    rows_at(upd, target * block, block),
                    out_ref.at[me],
                    u_sem,
                    target // NY,
                    target % NY,
                )
                return inner

            lax.fori_loop(0, tile // block, one, 0)
            return carry

        lax.fori_loop(0, padded // tile, make_gram, 0)
        lax.fori_loop(0, padded // tile, make_poly, 0)
        lax.fori_loop(0, tiles, make_iterate, 0)

    section_copy.wait_send()
    others = n_dp - 1
    take(mrecv.at[pl.ds(0, others * block)], m_sem.at[0])
    take(grecv.at[pl.ds(0, others * CAP)], g_sem.at[0])
    take(pmsend.at[pl.ds(0, (nz - 1) * PAD)], p_sem.at[0])
    take(frecv.at[pl.ds(0, nz * (NY - 1) * CAP)], y_sem.at[0])
    for di, d, count in directions:
        for step in range(count):
            ring_copy(di, d, step).wait_send()
    take(upd.at[pl.ds(0, others * block)], u_sem.at[0])
    take(out_ref, u_sem.at[1])


def on_device(section_rows, embedded, norm_gain, routes, out_grad, momentum):
    n_dp = lax.axis_size("dp")
    n_sec = lax.axis_size("section")
    nz = n_dp // NY
    half = nz // 2
    tokens, top, hidden = out_grad.shape[1:]
    experts, block = momentum.shape[1:3]
    width = norm_gain.shape[1]
    padded = -(-hidden // 256) * 256
    main = hidden // LANES * LANES
    slots = n_dp * CAP
    vmem = pl.BlockSpec(memory_space=pltpu.VMEM)
    pair = pltpu.SemaphoreType.DMA((2,))
    return pl.pallas_call(
        functools.partial(kernel, n_dp, n_sec),
        out_shape=jax.ShapeDtypeStruct((experts, block, hidden), BF16),
        in_specs=[vmem] * 6,
        out_specs=vmem,
        scratch_shapes=[
            pltpu.VMEM(section_rows.shape[1:], BF16),
            pltpu.VMEM((nz * tokens, width), BF16),
            pltpu.VMEM((top, nz * PAD, tokens), BF16),
            pltpu.VMEM((nz * PAD, tokens), F32),
            pltpu.VMEM((nz * PAD, tokens), F32),
            pltpu.VMEM((top * tokens, padded), BF16),
            pltpu.VMEM((slots, padded), BF16),
            pltpu.VMEM((n_dp * block, main), BF16),
            pltpu.VMEM((slots, padded), BF16),
            pltpu.VMEM((slots, width), BF16),
            pltpu.VMEM((slots, width), BF16),
            pltpu.VMEM((width, padded), F32),
            pltpu.VMEM((width, padded), BF16),
            pltpu.VMEM((padded, padded), BF16),
            pltpu.VMEM((padded, padded), BF16),
            pltpu.VMEM((width, hidden), BF16),
            pair,
            pair,
            pair,
            pair,
            pair,
            pair,
            pltpu.SemaphoreType.DMA((2, half)),
            pltpu.SemaphoreType.DMA((2, half)),
        ],
        compiler_params=pltpu.CompilerParams(
            collective_id=0, has_side_effects=True, vmem_limit_bytes=56 * 1024 * 1024
        ),
        name="muon_update",
    )(
        section_rows[0],
        embedded,
        norm_gain,
        routes[0].T,
        jnp.transpose(out_grad[0], (1, 2, 0)),
        momentum[0],
    )[None]


def solution(mesh):
    in_specs = (
        P("section", "dp", None),
        P("dp", None),
        P("section", None),
        P("section", "dp", None),
        P("section", "dp", None, None),
        P("section", None, "dp", None),
    )
    out_specs = P("section", None, "dp", None)
    return jax.shard_map(
        on_device, mesh=mesh, in_specs=in_specs, out_specs=out_specs, check_vma=False
    )
```

time: 428 us -> 295 us (0.69)
  the two profiles are of different devices: /device:TPU:2 before, /device:TPU:38 now
where the time goes in v1:
time: 295 us; the launch traced here: 294 us
  Pallas kernels  291 us (99%)
  local copies, waits for them, and re-layouts  3.93 us (1%)
    pallas_call x1, Pallas kernels, on_device(): pl.pallas_call(functools.partial(kernel, n_dp, n_sec), out_shape=jax.Shap...  291 us

profile of v1, /device:TPU:38, one launch (start us, length us, event | category | flops | bytes accessed | tf_op | source)
XLA Modules:
  0.0 294.5 jit_solution(4538425741047449948)
XLA Ops:
  0.0 1.3 copy.9
  1.3 290.5 %muon_update.1 = bf16[64,16,704]{2,1,0:T(8,128)(2,1)} custom-call(bf16[128,2048]{1,0:T(8,128)(2,1)} %bitcast.14, bf16[128,2048]{1,0:T(8,128)(2,1)} %emb_ref.1, f32[1,1024]{1,0:T(1,128)} %gain_ref.1, s32[6,128]{1,0:T(8,128)} %bitcast.15, bf16[6,704,128]{2,1,0:T(8,128)(2,1)} %bitcast.13, bf16[64,16,704]{2,1,0:T(8,128)(2,1)} %bitcast.12), custom_call_target="tpu_custom_call" | custom-call | tf_op jit(solution)/shard_map/muon_update/pallas_call | solution.py:409
  291.8 2.7 copy.11

commit v2 on v1

--- a/solution.py
+++ b/solution.py
@@ -23,6 +23,8 @@
 CAP = 16
 PAD = 8
 LANES = 128
+
+SCHEDULE = (32, 64, 64, 64, 64, 64, 64, 80, 96, 112, 128)
 
 
 def iota(shape, dim):
@@ -55,12 +57,15 @@
     gram,
     poly,
     upd,
+    tails_out,
+    tails_in,
     x_sem,
     m_sem,
     g_sem,
     p_sem,
     y_sem,
     u_sem,
+    t_sem,
     ring_send,
     ring_recv,
 ):
@@ -103,12 +108,14 @@
     before = lax.rem(sec + n_sec - 1, n_sec)
 
     def greet(k, carry):
+        step = (k + 1) // 2
+        to = me + n_dp // 2 + jnp.where(k % 2 == 1, step, n_dp - step)
         pl.semaphore_signal(
-            barrier, inc=1, device_id=(lax.rem(me + k, n_dp), sec), device_id_type=MESH
+            barrier, inc=1, device_id=(lax.rem(to, n_dp), sec), device_id_type=MESH
         )
         return carry
 
-    lax.fori_loop(1, n_dp, greet, 0)
+    lax.fori_loop(0, n_dp - 1, greet, 0)
     for other in (after, before):
         pl.semaphore_signal(barrier, inc=1, device_id=(me, other), device_id_type=MESH)
     pl.semaphore_wait(barrier, n_dp + 1)
@@ -143,33 +150,43 @@
         def _():
             pltpu.make_async_copy(src, dst, sems.at[1]).start()
 
-    def send_momentum(phase, lo, hi):
-        def one(j, carry):
-            to_z = wrap(z + offset(phase, j // NY))
-            to_y = lax.rem(y + j % NY, NY)
-            send_to(
-                mom_ref.at[to_z * NY + to_y, :, pl.ds(0, main)],
-                rows_at(mrecv, block * me, block),
-                m_sem,
-                to_z,
-                to_y,
-            )
-            return carry
-
-        lax.fori_loop(lo, hi, one, 0)
-
-    send_momentum(0, 0, half * NY)
+    share = half * NY
+
+    def stream(lo, hi):
+        for part in range(4):
+            first, last = max(lo, part * share), min(hi, (part + 1) * share)
+            if first < last:
+                lax.fori_loop(
+                    first - part * share,
+                    last - part * share,
+                    functools.partial(send_block, part // 2, part % 2 == 1),
+                    0,
+                )
+
+    def send_block(phase, cotangents, j, carry):
+        to_z = wrap(z + offset(phase, j // NY))
+        if cotangents:
+            to_y = j % NY
+            src = rows_at(gsend, (phase * share + j) * CAP, CAP)
+            send_to(src, rows_at(grecv, CAP * me, CAP), g_sem, to_z, to_y)
+        else:
+            to_y = lax.rem(y + j, NY)
+            src = mom_ref.at[to_z * NY + to_y, :, pl.ds(0, main)]
+            send_to(src, rows_at(mrecv, block * me, block), m_sem, to_z, to_y)
+        return carry
+
+    stream(0, SCHEDULE[0])
 
     table = nz * PAD
     expert = iota((table, tokens), 0)
     expert = jnp.where(expert % PAD < NY, (expert // PAD) * NY + expert % PAD, -1)
     named = jnp.zeros((table, tokens), F32)
     for k in range(top):
-        named += jnp.where(routes_ref[k : k + 1, :] == expert, 1.0, 0.0)
+        named += jnp.where(routes_ref[k] == expert, 1.0, 0.0)
     earlier = jnp.where(iota((tokens, tokens), 0) < iota((tokens, tokens), 1), 1.0, 0.0)
     place = jnp.dot(named.astype(BF16), earlier.astype(BF16), preferred_element_type=F32)
     for k in range(top):
-        wk[k] = jnp.where(routes_ref[k : k + 1, :] == expert, place, -1.0).astype(BF16)
+        wk[k] = jnp.where(routes_ref[k] == expert, place, -1.0).astype(BF16)
     pmsend[...] = jnp.where(named > 0.0, place, -1.0)
 
     def send_places(dz, carry):
@@ -184,33 +201,6 @@
             [gt_ref[k], jnp.zeros((padded - hidden, tokens), BF16)], axis=0
         )
         gsc[k * tokens : (k + 1) * tokens, :] = widened.T
-
-    section_copy.wait_recv()
-    values = jnp.where(sec == 0, emb_ref[...], rrecv[...]).astype(F32)
-    inverse = lax.rsqrt(jnp.mean(values * values, axis=-1, keepdims=True) + NORM_EPS)
-    fall[pl.ds(pl.multiple_of(z * tokens, tokens), tokens), :] = (
-        values[:, :width] * inverse * gain_ref[...]
-    ).astype(BF16)
-
-    directions = ((0, 1, half), (1, -1, half - 1))
-
-    def ring_copy(di, d, step):
-        part = rows_at(fall, wrap(z - d * step) * tokens, tokens)
-        return pltpu.make_async_remote_copy(
-            src_ref=part,
-            dst_ref=part,
-            send_sem=ring_send.at[di, step],
-            recv_sem=ring_recv.at[di, step],
-            device_id=(wrap(z + d) * NY + y, sec),
-            device_id_type=MESH,
-        )
-
-    def ring_step(step):
-        for di, d, count in directions:
-            if 1 <= step <= count:
-                ring_copy(di, d, step - 1).wait_recv()
-            if step < count:
-                ring_copy(di, d, step).start()
 
     slots = 4 * group
     shift = jnp.where(
@@ -245,19 +235,43 @@
             chosen[:, main:] + jnp.dot(tails, shift, preferred_element_type=F32)
         ).astype(BF16)
 
-        def one(j, carry):
-            to_z = wrap(z + offset(phase, 4 * q + j // NY))
-            to_y = j % NY
-            send_to(
-                rows_at(gsend, base + j * CAP, CAP),
-                rows_at(grecv, CAP * me, CAP),
-                g_sem,
-                to_z,
-                to_y,
-            )
-            return carry
-
-        lax.fori_loop(0, 4 * NY, one, 0)
+    for phase in range(2):
+        for q in range(chunks):
+            pack(phase, q)
+    stream(SCHEDULE[0], SCHEDULE[1])
+
+    section_copy.wait_recv()
+    values = jnp.where(sec == 0, emb_ref[...], rrecv[...]).astype(F32)
+    inverse = lax.rsqrt(jnp.mean(values * values, axis=-1, keepdims=True) + NORM_EPS)
+    fall[pl.ds(pl.multiple_of(z * tokens, tokens), tokens), :] = (
+        values[:, :width] * inverse * gain_ref[...]
+    ).astype(BF16)
+
+    parts = 2
+    piece = tokens // parts
+    ways = tuple(
+        (part, way, sign, half - (part + way) % 2)
+        for part in range(parts)
+        for way, sign in ((0, 1), (1, -1))
+    )
+
+    def ring_copy(part, way, sign, step):
+        held = rows_at(fall, wrap(z - sign * step) * tokens + part * piece, piece)
+        return pltpu.make_async_remote_copy(
+            src_ref=held,
+            dst_ref=held,
+            send_sem=ring_send.at[2 * part + way, step],
+            recv_sem=ring_recv.at[2 * part + way, step],
+            device_id=(wrap(z + sign) * NY + y, sec),
+            device_id_type=MESH,
+        )
+
+    def ring_step(step):
+        for part, way, sign, count in ways:
+            if 1 <= step <= count:
+                ring_copy(part, way, sign, step - 1).wait_recv()
+            if step < count:
+                ring_copy(part, way, sign, step).start()
 
     def pick(source):
         places = pmrecv[pl.ds(pl.multiple_of(source * PAD, PAD), PAD), :]
@@ -285,18 +299,12 @@
         if 0 < step < half:
             pick(wrap(z - step))
 
-    fillers = [functools.partial(pack, 0, q) for q in range(chunks)]
-    fillers.append(functools.partial(send_momentum, 1, 0, half * NY))
-    fillers += [functools.partial(pack, 1, q) for q in range(chunks)]
-    slots_for = {1: 0, 3: 1, 5: 2, 6: 3, 7: 4}
     for step in range(half + 1):
         ring_step(step)
         if step == 0:
             take(pmrecv, p_sem.at[1])
         pick_step(step)
-        for at_step, index in slots_for.items():
-            if min(at_step, half) == step and index < len(fillers):
-                fillers[index]()
+        stream(SCHEDULE[step + 1], SCHEDULE[step + 2])
 
     take(frecv, y_sem.at[1])
     take(grecv, g_sem.at[1])
@@ -360,17 +368,23 @@
             if not last_one:
                 xs[rows, :] = fresh
                 return carry
-            upd[rows, :] = (factor * fresh.astype(F32)).astype(BF16)[:, :hidden]
+            final = factor * fresh.astype(F32)
+            upd[rows, :] = final[:, :main].astype(BF16)
+            ends = final[:, main:].reshape(tile // block, 2, block // 2, LANES)
+            ends = ends[:, 0] + pltpu.roll(ends[:, 1], tail, 2)
+            tails_out[pl.ds(t * (tile // block), tile // block)] = ends.astype(BF16)
 
             def one(j, inner):
                 target = t * (tile // block) + j
+                to_z, to_y = target // NY, target % NY
                 send_to(
                     rows_at(upd, target * block, block),
-                    out_ref.at[me],
+                    out_ref.at[me, :, pl.ds(0, main)],
                     u_sem,
-                    target // NY,
-                    target % NY,
+                    to_z,
+                    to_y,
                 )
+                send_to(tails_out.at[target], tails_in.at[me], t_sem, to_z, to_y)
                 return inner
 
             lax.fori_loop(0, tile // block, one, 0)
@@ -386,11 +400,16 @@
     take(grecv.at[pl.ds(0, others * CAP)], g_sem.at[0])
     take(pmsend.at[pl.ds(0, (nz - 1) * PAD)], p_sem.at[0])
     take(frecv.at[pl.ds(0, nz * (NY - 1) * CAP)], y_sem.at[0])
-    for di, d, count in directions:
+    for part, way, sign, count in ways:
         for step in range(count):
-            ring_copy(di, d, step).wait_send()
+            ring_copy(part, way, sign, step).wait_send()
     take(upd.at[pl.ds(0, others * block)], u_sem.at[0])
-    take(out_ref, u_sem.at[1])
+    take(tails_out.at[pl.ds(0, others)], t_sem.at[0])
+    take(tails_in, t_sem.at[1])
+    take(out_ref.at[:, :, pl.ds(0, main)], u_sem.at[1])
+    ends = tails_in[...].astype(F32)
+    ends = jnp.concatenate([ends, pltpu.roll(ends, tail, 2)], axis=1)
+    out_ref[:, :, main:] = ends[:, :, :tail].astype(BF16)
 
 
 def on_device(section_rows, embedded, norm_gain, routes, out_grad, momentum):
@@ -427,15 +446,18 @@
             pltpu.VMEM((width, padded), BF16),
             pltpu.VMEM((padded, padded), BF16),
             pltpu.VMEM((padded, padded), BF16),
-            pltpu.VMEM((width, hidden), BF16),
-            pair,
-            pair,
-            pair,
-            pair,
-            pair,
-            pair,
-            pltpu.SemaphoreType.DMA((2, half)),
-            pltpu.SemaphoreType.DMA((2, half)),
+            pltpu.VMEM((width, main), BF16),
+            pltpu.VMEM((n_dp, block // 2, LANES), BF16),
+            pltpu.VMEM((n_dp, block // 2, LANES), BF16),
+            pair,
+            pair,
+            pair,
+            pair,
+            pair,
+            pair,
+            pair,
+            pltpu.SemaphoreType.DMA((4, half)),
+            pltpu.SemaphoreType.DMA((4, half)),
         ],
         compiler_params=pltpu.CompilerParams(
             collective_id=0, has_side_effects=True, vmem_limit_bytes=56 * 1024 * 1024
@@ -445,7 +467,7 @@
         section_rows[0],
         embedded,
         norm_gain,
-        routes[0].T,
+        jnp.transpose(routes, (2, 0, 1)),
         jnp.transpose(out_grad[0], (1, 2, 0)),
         momentum[0],
     )[None]

time: 295 us -> 289 us (0.980)
  the two profiles are of different devices: /device:TPU:38 before, /device:TPU:102 now
where the time goes in v2:
time: 289 us
  Pallas kernels  286 us (99%)
    pallas_call x1, Pallas kernels, on_device(): pl.pallas_call(functools.partial(kernel, n_dp, n_sec), out_shape=jax.Shap...  286 us

profile of v2, /device:TPU:102, one launch (start us, length us, event | category | flops | bytes accessed | tf_op | source)
XLA Modules:
  0.0 288.8 jit_solution(6592371122698524250)
XLA Ops:
  0.0 286.1 %muon_update.1 = bf16[64,16,704]{2,1,0:T(8,128)(2,1)} custom-call(bf16[128,2048]{1,0:T(8,128)(2,1)} %bitcast.10, bf16[128,2048]{1,0:T(8,128)(2,1)} %emb_ref.1, f32[1,1024]{1,0:T(1,128)} %gain_ref.1, s32[6,1,128]{2,1,0:T(1,128)} %bitcast.11, bf16[6,704,128]{2,1,0:T(8,128)(2,1)} %bitcast.9, bf16[64,16,704]{2,1,0:T(8,128)(2,1)} %bitcast.8), custom_call_target="tpu_custom_call" | custom-call | tf_op jit(solution)/shard_map/muon_update/pallas_call | solution.py:428
  286.2 2.7 copy.8

commit v3 on v2

--- a/solution.py
+++ b/solution.py
@@ -24,7 +24,7 @@
 PAD = 8
 LANES = 128
 
-SCHEDULE = (32, 64, 64, 64, 64, 64, 64, 80, 96, 112, 128)
+SCHEDULE = (32, 32, 40, 48, 56, 64, 68, 72, 76, 80, 128)
 
 
 def iota(shape, dim):

time: 289 us -> 286 us (0.990)
  the two profiles are of different devices: /device:TPU:102 before, /device:TPU:126 now
where the time goes in v3:
time: 286 us
  Pallas kernels  283 us (99%)
    pallas_call x1, Pallas kernels, on_device(): pl.pallas_call(functools.partial(kernel, n_dp, n_sec), out_shape=jax.Shap...  283 us

profile of v3, /device:TPU:126, one launch (start us, length us, event | category | flops | bytes accessed | tf_op | source)
XLA Modules:
  0.0 285.5 jit_solution(5708598366771328077)
XLA Ops:
  0.0 282.8 %muon_update.1 = bf16[64,16,704]{2,1,0:T(8,128)(2,1)} custom-call(bf16[128,2048]{1,0:T(8,128)(2,1)} %bitcast.10, bf16[128,2048]{1,0:T(8,128)(2,1)} %emb_ref.1, f32[1,1024]{1,0:T(1,128)} %gain_ref.1, s32[6,1,128]{2,1,0:T(1,128)} %bitcast.11, bf16[6,704,128]{2,1,0:T(8,128)(2,1)} %bitcast.9, bf16[64,16,704]{2,1,0:T(8,128)(2,1)} %bitcast.8), custom_call_target="tpu_custom_call" | custom-call | tf_op jit(solution)/shard_map/muon_update/pallas_call | solution.py:428
  282.9 2.7 copy.8
